TPU v7x, 32 devices: a whole 2x2x4 slice. The times are simulated.
32 devices in a mesh: snd: 8 (over z, y), map: 4 (over x, core).
Axes of the slice: x: 2, y: 2, z: 4, core: 2. Of those that a mesh axis runs over, the one named last changes fastest.
Arguments:
- sensitivity_blocks: bfloat16 [4096, 128, 128], P(('snd', 'map')), may hold values from -0.1875 to 0.1875
- block_placement_table: int32 [3, 4096], P(None, ('snd', 'map')), may hold values from 0 to 63, as said below
- needed_tile_lists: int32 [256, 4], P(('snd', 'map')), may hold values from -1 to 127, as said below
- location_category: int32 [32768], P('map'), may hold values from 0 to 15
- ground_warmth_celsius: float32 [16, 32768], P('snd', 'map'), may hold values from -5 to 30
- wetness_factor: float32 [16, 32768], P('snd', 'map'), may hold values from 0.2 to 1
- carbon_reservoirs: float32 [3, 32768], P(None, 'map'), may hold values from 0.2 to 3
- category_sensitivity_effect: float32 [16], replicated, may hold values from -4 to 4
- reservoir_decay_effect: float32 [3, 16], replicated, may hold values from -4 to 4
- measured_anomaly: float32 [512, 128], P(('snd', 'map')), may hold values from -6 to 6
- retrieval_precision: float32 [512, 128], P(('snd', 'map')), may hold values from 0.5 to 2
Outputs:
- model_xco2: float32 [512, 128], P(('snd', 'map'))
- flux_grad: float32 [16, 32768], P('snd', 'map')
- class_grad: float32 [4, 16], replicated
- cost: float32 [], replicated
Inputs may be any that keep to these rules, and one draw needn't show every extreme that they name: `block_placement_table`: row 0 is a block row below 64, row 1 a cell tile below 64, row 2 a slot below 16; each block's tile appears in its device's request list to the owner of its slot (slot // 2) as (slot % 2) * 64 + tile. `needed_tile_lists`: row o of a device's 8 rows lists distinct local tile ids of owner o followed by -1; every list has 1 to 4 ids, and on every device some list has exactly 4.
All inputs are finite; a program needn't handle non-finite values.
Results may differ from a plain program's by a relative error of at most 0.0039.
Values may be sent and summed in bfloat16 or wider, within the bound.
A program may use at most 64 MiB of HBM per device.

v0:
```python
import jax
import jax.numpy as jnp
from jax import lax
from jax.sharding import PartitionSpec as P

BASELINE_CELSIUS = 15.0
LOG_BASE_Q = 0.6931471805599453
PRIOR_VAR = 0.09


def ground_efflux_forward(
    ground_warmth_celsius,
    wetness_factor,
    carbon_reservoirs,
    location_category,
    category_sensitivity_effect,
    reservoir_decay_effect,
):
    nclass = category_sensitivity_effect.shape[0]
    category_onehot = (
        location_category[None, :] == jnp.arange(nclass, dtype=jnp.int32)[:, None]
    ).astype(jnp.float32)
    log_q = (
        LOG_BASE_Q
        + jnp.dot(
            category_sensitivity_effect[None, :], category_onehot, precision=lax.Precision.HIGHEST
        )[0]
    )
    base = jnp.array([0.6, 0.25, 0.1], dtype=jnp.float32)
    rates = base[:, None] * jnp.exp(
        jnp.dot(reservoir_decay_effect, category_onehot, precision=lax.Precision.HIGHEST)
    )
    decay_lifetime = (ground_warmth_celsius - BASELINE_CELSIUS) / 10.0
    modifier = jnp.exp(log_q[None, :] * decay_lifetime) * wetness_factor
    device_number = (rates * carbon_reservoirs)[:, None, :] * modifier[None]
    return (category_onehot, decay_lifetime, device_number)


def shards(
    sensitivity_blocks,
    block_placement_table,
    needed_tile_lists,
    location_category,
    ground_warmth_celsius,
    wetness_factor,
    carbon_reservoirs,
    category_sensitivity_effect,
    reservoir_decay_effect,
    measured_anomaly,
    retrieval_precision,
):
    tile = sensitivity_blocks.shape[1]
    epochs_each_device, locations_each_device = ground_warmth_celsius.shape
    tiles_dev = locations_each_device // tile
    n_snd = lax.axis_size("snd")
    rows_dev = measured_anomaly.shape[0] * lax.axis_size("map")
    category_onehot, decay_lifetime, device_number = ground_efflux_forward(
        ground_warmth_celsius,
        wetness_factor,
        carbon_reservoirs,
        location_category,
        category_sensitivity_effect,
        reservoir_decay_effect,
    )
    flux = device_number[0] + device_number[1] + device_number[2]
    flux_low = flux.astype(jnp.bfloat16)
    block_row = block_placement_table[0]
    block_tile = block_placement_table[1]
    block_slot = block_placement_table[2]
    everything = lax.all_gather(flux_low, "snd", axis=0, tiled=True)
    position = block_slot * tiles_dev + block_tile
    vectors = jnp.take(
        everything.reshape(n_snd * epochs_each_device * tiles_dev, tile), position, axis=0
    )
    contrib = jnp.einsum(
        "bij,bj->bi", sensitivity_blocks, vectors, preferred_element_type=jnp.float32
    )
    row_hot = (jnp.arange(rows_dev, dtype=jnp.int32)[:, None] == block_row[None, :]).astype(
        jnp.float32
    )
    partial_rows = jnp.dot(row_hot, contrib, precision=lax.Precision.HIGHEST)
    model_xco2 = lax.psum_scatter(partial_rows, "map", scatter_dimension=0, tiled=True)
    diff = model_xco2 - measured_anomaly
    weighted = (diff * retrieval_precision).astype(jnp.bfloat16)
    misfit = 0.5 * jnp.sum(retrieval_precision * diff * diff)
    spread = lax.all_gather(weighted, "map", axis=0, tiled=True)
    back_rows = jnp.take(spread, block_row, axis=0)
    block_grads = jnp.einsum(
        "bij,bi->bj", sensitivity_blocks, back_rows, preferred_element_type=jnp.float32
    )
    dense = jax.ops.segment_sum(
        block_grads, position, num_segments=n_snd * epochs_each_device * tiles_dev
    )
    flux_grad = lax.psum_scatter(
        dense.reshape(n_snd * epochs_each_device, locations_each_device),
        "snd",
        scatter_dimension=0,
        tiled=True,
    )
    terms = jnp.stack(
        [
            jnp.sum(flux_grad * flux * decay_lifetime, axis=0),
            jnp.sum(flux_grad * device_number[0], axis=0),
            jnp.sum(flux_grad * device_number[1], axis=0),
            jnp.sum(flux_grad * device_number[2], axis=0),
        ]
    )
    class_part = jnp.dot(terms, category_onehot.T, precision=lax.Precision.HIGHEST)
    total_misfit = lax.psum(misfit, ("snd", "map"))
    class_total = lax.psum(class_part, ("snd", "map"))
    prior = (
        jnp.concatenate([category_sensitivity_effect[None, :], reservoir_decay_effect], axis=0)
        / PRIOR_VAR
    )
    class_grad = class_total + prior
    cost = (
        total_misfit
        + 0.5 * jnp.sum(category_sensitivity_effect * category_sensitivity_effect) / PRIOR_VAR
        + 0.5 * jnp.sum(reservoir_decay_effect * reservoir_decay_effect) / PRIOR_VAR
    )
    return (model_xco2, flux_grad, class_grad, cost)


def solution(mesh):
    in_specs = (
        P(("snd", "map"), None, None),
        P(None, ("snd", "map")),
        P(("snd", "map"), None),
        P("map"),
        P("snd", "map"),
        P("snd", "map"),
        P(None, "map"),
        P(),
        P(),
        P(("snd", "map"), None),
        P(("snd", "map"), None),
    )
    out_specs = (P(("snd", "map"), None), P("snd", "map"), P(), P())
    return jax.shard_map(shards, mesh=mesh, in_specs=in_specs, out_specs=out_specs, check_vma=False)
```

profile of v0, /device:TPU:0, one launch (start us, length us, event | category | flops | bytes accessed | tf_op | source)
XLA Modules:
  0.0 207.9 jit_solution(8074908913130257089)
XLA Ops:
  7.2 0.0 copy-start.1
  7.2 0.0 copy-start.2
  7.2 0.0 reduce-scatter.2.cloned.1.call-start
  7.2 0.8 compare_and_fusion.1
  8.0 0.7 slice_bitcast_fusion.3
  8.7 1.0 fusion.4
  9.8 0.9 exponential_multiply_fusion
  10.7 1.2 fusion.2
  12.0 0.1 broadcast_multiply_fusion
  12.1 0.1 convert_bitcast_fusion
  12.1 32.5 %all-gather = bf16[8,2,8192]{2,1,0:T(2,128)(2,1)S(1)} all-gather(bf16[1,2,8192]{2,1,0:T(2,128)(2,1)S(1)} %get-tuple-element.13), channel_id=1, replica_groups=mesh['snd'=8,'map'=4] {'snd'}, dimensions={0}, use_global_device_ids=true | all-gather | bytes 294912 | tf_op jit(solution)/shard_map/all_gather | solution.py:70
  44.6 0.2 reshape.110
  44.9 0.7 gather_fusion
  45.6 0.1 select_bitcast_fusion.1
  45.7 4.4 %fusion.19 = f32[128,1,128]{2,1,0:T(1,128)S(1)} fusion(bf16[128,128,128]{2,1,0:T(8,128)(2,1)} %param.12, bf16[128,128,1]{1,0,2:T(8,128)(2,1)S(1)} %select_bitcast_fusion.1), kind=kOutput, calls=%fused_computation.28 | convolution fusion | flops 4194304 | bytes 4292608 | tf_op jit(solution)/shard_map/bij,bj->bi/dot_general | solution.py:75
  50.1 0.0 copy-start.4
  50.1 0.0 copy-start.3
  50.1 0.0 copy-start.6
  50.1 0.0 copy-start
  50.2 0.0 copy-start.5
  50.2 0.8 fusion.21
  51.0 0.0 reduce-scatter.2.cloned.1.call-update
  51.0 0.0 all-reduce.4.cloned.1.call-start
  51.0 0.7 fusion.25
  51.7 19.7 %reduce-scatter.2.cloned.1.call-done = f32[16,128]{1,0:T(8,128)} async-done(((f32[64,128]{1,0:T(8,128)}), f32[16,128]{1,0:T(8,128)}) %reduce-scatter.2.cloned.1.call-update) | async-done | bytes 8208 | tf_op jit(solution)/shard_map/reduce_scatter | solution.py:82
  71.5 0.0 copy-done.1
  71.5 0.0 copy-done.2
  71.5 1.3 multiply_reduce_fusion.4
  72.8 5.2 %all_gather.7 = bf16[64,128]{1,0:T(8,128)(2,1)S(1)} all-gather(bf16[16,128]{1,0:T(8,128)(2,1)S(1)} %get-tuple-element.16), channel_id=1, replica_groups=mesh['snd'=8,'map'=4] {'map'}, dimensions={0}, use_global_device_ids=true | all-gather | bytes 20480 | tf_op jit(solution)/shard_map/all_gather | solution.py:86
  77.9 0.7 gather_fusion.1
  78.7 0.1 select_bitcast_fusion
  78.7 3.4 %fusion.17 = f32[128,1,128]{2,1,0:T(1,128)S(1)} fusion(bf16[128,128,128]{2,1,0:T(8,128)(2,1)} %param.12, bf16[128,128,1]{1,0,2:T(8,128)(2,1)S(1)} %select_bitcast_fusion), kind=kOutput, calls=%fused_computation.26 | convolution fusion | flops 4194304 | bytes 4292608 | tf_op jit(solution)/shard_map/bij,bi->bj/dot_general | solution.py:88
  82.1 1.2 scatter_custom_fusion
  83.3 0.9 reshape.111
  84.2 0.0 all-reduce.4.cloned.1.call-update
  84.2 0.0 copy-done.4
  84.2 0.6 multiply_reduce_fusion.6
  85.5 0.0 copy-done.3
  85.5 0.6 multiply_reduce_fusion.5
  86.7 0.0 copy-done.6
  86.8 0.6 dynamic-slice
  88.6 68.1 %all-reduce.4.cloned.1.call-done = f32[16,8192]{1,0:T(8,128)} async-done(((f32[16,8192]{1,0:T(8,128)}), f32[16,8192]{1,0:T(8,128)}) %all-reduce.4.cloned.1.call-update) | async-done | bytes 524304
  156.8 0.0 copy-done
  156.8 1.7 multiply_reduce_fusion.2
  158.5 0.0 copy-done.5
  158.5 0.5 fusion.3
  159.0 39.6 %all-reduce.1 = (f32[4,16]{1,0:T(4,128)S(1)}, f32[]{:T(128)}) all-reduce(f32[4,16]{1,0:T(4,128)S(1)} %fusion.3, f32[]{:T(128)S(6)} %mul.123), channel_id=1, replica_groups=mesh['snd'=8,'map'=4] {'snd','map'}, use_global_device_ids=true, to_apply=%region_7.8 | all-reduce | flops 65 | bytes 520 | tf_op jit(solution)/shard_map/psum | solution.py:110
  198.7 0.6 fusion.23
  (4 shorter events, 0.0 us)
Async XLA Ops:
  7.2 64.3 %copy-start.1 = (f32[16,128]{1,0:T(8,128)S(1)}, f32[16,128]{1,0:T(8,128)}, u32[]{:S(2)}) copy-start(f32[16,128]{1,0:T(8,128)} %param.21) | copy-start | bytes 24580
  7.2 64.3 %copy-start.2 = (f32[16,128]{1,0:T(8,128)S(1)}, f32[16,128]{1,0:T(8,128)}, u32[]{:S(2)}) copy-start(f32[16,128]{1,0:T(8,128)} %param.20) | copy-start | bytes 24580
  7.2 64.3 %reduce-scatter.2.cloned.1.call-start = ((), (), s32[]{:S(2)}) async-start(), calls=%async_computation.1 | async-start | bytes 40960 | tf_op jit(solution)/shard_map/reduce_scatter | solution.py:82
  50.1 34.1 %copy-start.4 = (f32[16]{0:T(128)S(1)}, f32[16]{0:T(128)}, u32[]{:S(2)}) copy-start(f32[16]{0:T(128)} %param.18) | copy-start | bytes 196
  50.1 35.4 %copy-start.3 = (f32[3,16]{1,0:T(4,128)S(1)}, f32[3,16]{1,0:T(4,128)}, u32[]{:S(2)}) copy-start(f32[3,16]{1,0:T(4,128)} %param.19) | copy-start | bytes 580
  50.1 36.6 %copy-start.6 = (u32[32]{0:T(128)S(1)}, u32[32]{0:T(128)}, u32[]{:S(2)}) copy-start(u32[32]{0:T(128)} %constant.62) | copy-start | bytes 388
  50.1 106.7 %copy-start = (f32[2,8192]{1,0:T(2,128)S(1)}, f32[2,8192]{1,0:T(2,128)}, u32[]{:S(2)}) copy-start(f32[2,8192]{1,0:T(2,128)} %param.15) | copy-start | bytes 196612
  50.2 108.4 %copy-start.5 = (s32[8192]{0:T(1024)S(1)}, s32[8192]{0:T(1024)}, u32[]{:S(2)}) copy-start(s32[8192]{0:T(1024)} %param.14) | copy-start | bytes 98308
  51.0 105.8 %all-reduce.4.cloned.1.call-start = ((), (), s32[]{:S(2)}) async-start(), calls=%async_computation.2 | async-start | bytes 1048576
Sparse Core Ops, SparseCore 0:
  51.1 20.3 reduce-scatter.1
  84.3 72.4 all-reduce.3
where the time goes:
time: 209 us; the launch traced here: 208 us
  waiting for transfers between devices  87.9 us (42%)
  blocking collectives  77.3 us (37%)
  between operations  18.6 us (9%)
  matrix products  11.4 us (5%)
  other arithmetic  8.75 us (4%)
  local copies, waits for them, and re-layouts  3.86 us (2%)
    unnamed x3, waiting for transfers between devices  68.2 us
    psum x1, blocking collectives, shards(): class_total = lax.psum(class_part, ('snd', 'map'))  39.6 us
    all_gather x1, blocking collectives, shards(): everything = lax.all_gather(flux_low, 'snd', axis=0, tiled=True)  32.5 us
    reduce_scatter x1, waiting for transfers between devices, shards(): lax.psum_scatter(partial_rows, 'map', scatter_dimension=0, tiled=True)  19.7 us
    all_gather x1, blocking collectives, shards(): spread = lax.all_gather(weighted, 'map', axis=0, tiled=True)  5.17 us
    dot_general x1, matrix products, shards(): jnp.einsum('bij,bj->bi', sensitivity_blocks, vectors, preferred_element_t...  4.43 us
  transfers between devices with their start and end apart: 2, of which 2 were waited for; matrix products, arithmetic and copies ran while one was open for 1% of the time, Pallas kernels for 0%

commit v1 on v0

v1 whole, which is shorter than its diff:
```python
import functools

import jax
import jax.numpy as jnp
from jax import lax
from jax.experimental import pallas as pl
from jax.experimental.pallas import tpu as pltpu
from jax.sharding import PartitionSpec as P

BASELINE_CELSIUS = 15.0
LOG_BASE_Q = 0.6931471805599453
PRIOR_VAR = 0.09
RATES = (0.6, 0.25, 0.1)
CHUNK = 8
F32 = jnp.float32
BF16 = jnp.bfloat16


def split3(x):
    hi = x.astype(BF16)
    rest = x - hi.astype(F32)
    mid = rest.astype(BF16)
    low = (rest - mid.astype(F32)).astype(BF16)
    return hi, mid, low


def dot(a, b, dims):
    return lax.dot_general(a, b, (dims, ((), ())), preferred_element_type=F32)


def onehot(mask):
    return jnp.where(mask, 1.0, 0.0).astype(BF16)


def pick(sel, x):
    hi, mid, low = split3(x)
    return (dot(sel, hi, ((1,), (0,))) + dot(sel, mid, ((1,), (0,)))) + dot(sel, low, ((1,), (0,)))


def iota(shape, dim):
    return lax.broadcasted_iota(jnp.int32, shape, dim)


def kernel(
    n_s, n_m, sens_hbm, table, lists, cat_hbm, warm_hbm, wet_hbm, carb_hbm, q_s, r_s, q_v, r_v, meas_hbm, prec_hbm,
    model_out, grad_out, class_out, cost_out,
    sens, cat, warm_in, wet_in, carb_in, warm, wet, carb,
    req_send, req_recv, rep_send, rep_recv, mbuf, part, gsend, grecv, tsend, trecv,
    ids, vecs, tcol, rcol, model, fg, srows,
    local_sem, s_req, r_req, s_rep, r_rep, s_m, r_m, s_p, r_p, s_g, r_g, s_t, r_t,
):
    cap = lists.shape[1]
    nreq = n_s * cap
    slots = warm_hbm.shape[0]
    tiles = cat.shape[0]
    nclass = q_s.shape[0]
    pools = carb_hbm.shape[0]
    rows = meas_hbm.shape[0]
    allrows = rows * n_m
    nb = table.shape[1]
    tile = sens.shape[1]
    me = lax.axis_index("snd")
    mm = lax.axis_index("map")
    snd_dev = lambda e: {"snd": lax.rem(me + e + n_s, n_s)}
    map_dev = lambda f: {"map": lax.rem(mm + f + n_m, n_m)}

    def remote(src, dst, ss, rs, dev):
        return pltpu.make_async_remote_copy(
            src_ref=src, dst_ref=dst, send_sem=ss, recv_sem=rs, device_id=dev, device_id_type=pl.DeviceIdType.MESH
        )

    barrier = pltpu.get_barrier_semaphore()
    for e in range(1, n_s):
        pl.semaphore_signal(barrier, inc=1, device_id=snd_dev(e), device_id_type=pl.DeviceIdType.MESH)
    for f in range(1, n_m):
        pl.semaphore_signal(barrier, inc=1, device_id=map_dev(f), device_id_type=pl.DeviceIdType.MESH)

    loads = [
        pltpu.make_async_copy(src, dst, local_sem.at[i])
        for i, (src, dst) in enumerate(
            [
                (warm_hbm, warm_in),
                (wet_hbm, wet_in),
                (carb_hbm, carb_in),
                (cat_hbm, cat),
                (meas_hbm, mbuf.at[0, 0]),
                (prec_hbm, mbuf.at[0, 1]),
                (sens_hbm, sens),
            ]
        )
    ]
    for load in loads:
        load.start()

    row_in = iota((cap, tile), 0)
    for e in range(n_s):
        owner = lax.rem(me + e, n_s)
        whole_id = jnp.full((cap, tile), -1, jnp.int32)
        spot = jnp.full((cap, tile), -1, jnp.int32)
        tile_id = jnp.full((cap, tile), -1, jnp.int32)
        for k in range(cap):
            asked = lists[owner, k]
            t = lax.rem(asked, tiles)
            here = row_in == k
            whole_id = jnp.where(here, jnp.where(asked < 0, -1, owner * (slots * tiles) + asked), whole_id)
            spot = jnp.where(here, t * slots + lax.div(asked, tiles), spot)
            tile_id = jnp.where(here, t, tile_id)
        if e == 0:
            req_recv[0] = spot
        else:
            req_send[e] = spot
        ids[0, pl.ds(e * cap, cap), :] = whole_id
        ids[1, pl.ds(e * cap, cap), :] = tile_id

    pl.semaphore_wait(barrier, n_s - 1 + n_m - 1)

    req = [remote(req_send.at[e], req_recv.at[e], s_req.at[e], r_req.at[e], snd_dev(e)) for e in range(1, n_s)]
    for c in req:
        c.start()
    obs = []
    for f in range(1, n_m):
        obs.append(remote(meas_hbm, mbuf.at[f, 0], s_m.at[f, 0], r_m.at[f, 0], map_dev(f)))
        obs.append(remote(prec_hbm, mbuf.at[f, 1], s_m.at[f, 1], r_m.at[f, 1], map_dev(f)))
    for c in obs:
        c.start()

    carb[...] = jnp.zeros_like(carb)
    for load in loads[:4]:
        load.wait()
    for t in range(tiles):
        lanes = pl.ds(t * tile, tile)
        warm[pl.ds(slots * t, slots), :] = warm_in[:, lanes]
        wet[pl.ds(slots * t, slots), :] = wet_in[:, lanes]
        carb[pl.ds(4 * t, pools), :] = carb_in[:, lanes]
    warm_parts = split3(warm[...])
    wet_parts = split3(wet[...])

    tile_id = ids[1]
    cls = dot(onehot(tile_id[:, :tiles] == iota((nreq, tiles), 1)), cat[...].astype(F32).astype(BF16), ((1,), (0,)))
    cls = cls.astype(jnp.int32)
    wide = jnp.concatenate([tile_id] * (4 * tiles // tile), axis=1)
    wide_at = iota((nreq, 4 * tiles), 1)
    log_q = jnp.zeros((nreq, tile), F32)
    effects = [jnp.zeros((nreq, tile), F32) for _ in range(pools)]
    for c in range(nclass):
        here = cls == c
        log_q = jnp.where(here, q_s[c], log_q)
        for p in range(pools):
            effects[p] = jnp.where(here, r_s[p, c], effects[p])
    log_q = LOG_BASE_Q + log_q
    held = []
    for p in range(pools):
        carbon = pick(onehot(wide * 4 + p == wide_at), carb[...])
        held.append(RATES[p] * jnp.exp(effects[p]) * carbon)

    block_row = table[0:1, :]
    block_id = table[2:3, :] * tiles + table[1:2, :]
    asked_hot = onehot(ids[0][:, :nb] == block_id)
    row_hot = onehot(iota((allrows, nb), 0) == block_row)
    tcol[...] = dot(asked_hot, iota((nreq, tile), 0).astype(F32).astype(BF16), ((0,), (0,)))
    rcol[...] = dot(row_hot, iota((allrows, tile), 0).astype(F32).astype(BF16), ((0,), (0,)))

    for c in req:
        c.wait_recv()
    for e in range(n_s):
        ids[0, pl.ds(e * cap, cap), :] = req_recv[e]
    sel = onehot(ids[0] == iota((nreq, tile), 1))
    every = dot(sel, jnp.concatenate(list(warm_parts) + list(wet_parts), axis=1), ((1,), (0,)))
    cut = [every[:, i * tile : (i + 1) * tile] for i in range(6)]
    out_warm = (cut[0] + cut[1]) + cut[2]
    out_wet = (cut[3] + cut[4]) + cut[5]
    rep = []
    for e in range(n_s):
        to = rep_recv if e == 0 else rep_send
        to[e, 0:cap, :] = out_warm[e * cap : (e + 1) * cap]
        to[e, cap : 2 * cap, :] = out_wet[e * cap : (e + 1) * cap]
        if e:
            rep.append(remote(rep_send.at[e], rep_recv.at[e], s_rep.at[e], r_rep.at[e], snd_dev(-e)))
            rep[-1].start()
    for c in rep:
        c.wait_recv()
    for e in range(n_s):
        vecs[0, pl.ds(e * cap, cap), :] = rep_recv[e, 0:cap, :]
        vecs[1, pl.ds(e * cap, cap), :] = rep_recv[e, cap : 2 * cap, :]

    tau = (vecs[0] - BASELINE_CELSIUS) / 10.0
    modifier = jnp.exp(log_q * tau) * vecs[1]
    pieces = [h * modifier for h in held]
    flux = pieces[0] + pieces[1] + pieces[2]
    flux_low = flux.astype(BF16)

    tcol_hot = onehot(tcol[:, :nreq] == iota((nb, nreq), 1).astype(F32))
    vecs_b = dot(tcol_hot, flux_low, ((1,), (0,)))
    model_at = iota((allrows, tile), 0).astype(F32)
    vb = fg
    vb[...] = vecs_b
    loads[6].wait()

    def forward(step, acc):
        at = pl.multiple_of(step * CHUNK, CHUNK)
        v = vb[pl.ds(at, CHUNK), :]
        r = rcol[pl.ds(at, CHUNK), :]
        left = [jnp.where(model_at == r[u : u + 1], v[u : u + 1], 0.0).astype(BF16) for u in range(CHUNK)]
        right = [
            sens[pl.ds(pl.multiple_of((step * CHUNK + u) * tile, tile), tile), :] for u in range(CHUNK)
        ]
        return acc + dot(jnp.concatenate(left, axis=1), jnp.concatenate(right, axis=1), ((1,), (1,)))

    part[0] = lax.fori_loop(0, nb // CHUNK, forward, jnp.zeros((allrows, tile), F32))

    swap = [remote(part.at[0], part.at[f], s_p.at[f], r_p.at[f], map_dev(f)) for f in range(1, n_m)]
    for c in swap:
        c.start()
    for c in loads[4:6]:
        c.wait()
    for c in obs:
        c.wait_recv()
    meas, prec = [], []
    for a in range(n_m):
        slot = lax.rem(mm - a + n_m, n_m)
        meas.append(mbuf[slot, 0])
        prec.append(mbuf[slot, 1])
    meas = jnp.concatenate(meas, axis=0)
    prec = jnp.concatenate(prec, axis=0)
    rcol_hot = onehot(rcol[:, :allrows] == iota((nb, allrows), 1).astype(F32))
    for c in swap:
        c.wait_recv()
    total = part[lax.rem(mm + n_m, n_m)]
    for a in range(1, n_m):
        total = total + part[lax.rem(mm - a + n_m, n_m)]
    model[...] = total
    diff = total - meas
    weighted = (diff * prec).astype(BF16)
    own = model[pl.ds(pl.multiple_of(mm * rows, rows), rows), :]
    model_out[...] = own
    own_diff = own - mbuf[0, 0]
    misfit = 0.5 * jnp.sum(mbuf[0, 1] * own_diff * own_diff, keepdims=True)

    vb[...] = dot(rcol_hot, weighted, ((1,), (0,)))
    asked_at = iota((nreq, tile), 0).astype(F32)

    def backward(step, acc):
        at = pl.multiple_of(step * CHUNK, CHUNK)
        v = vb[pl.ds(at, CHUNK), :]
        r = tcol[pl.ds(at, CHUNK), :]
        left = [jnp.where(asked_at == r[u : u + 1], v[u : u + 1], 0.0).astype(BF16) for u in range(CHUNK)]
        right = sens[pl.ds(pl.multiple_of(step * CHUNK * tile, CHUNK * tile), CHUNK * tile), :]
        return acc + dot(jnp.concatenate(left, axis=1), right, ((1,), (0,)))

    grads = lax.fori_loop(0, nb // CHUNK, backward, jnp.zeros((nreq, tile), F32))

    terms = [grads * flux * tau] + [grads * piece for piece in pieces]
    for c in range(nclass):
        here = cls == c
        for p, term in enumerate(terms):
            srows[pl.ds(p * nclass + c, 1), :] = jnp.sum(jnp.where(here, term, 0.0), axis=0, keepdims=True)
    sums = jnp.sum(srows[...], axis=1, keepdims=True)
    diagonal = iota((nclass, tile), 0) == iota((nclass, tile), 1)
    lines = []
    for p in range(1 + pools):
        line = jnp.sum(jnp.where(diagonal, sums[p * nclass : (p + 1) * nclass], 0.0), axis=0, keepdims=True)
        if p == 0:
            line = jnp.where(iota((1, tile), 1) == nclass, misfit, line)
        lines.append(line)
    share = jnp.concatenate(lines, axis=0)
    back = []
    for e in range(n_s):
        to = grecv if e == 0 else gsend
        to[e, 0:cap, :] = grads[e * cap : (e + 1) * cap]
        to[e, cap:, :] = share
        if e:
            back.append(remote(gsend.at[e], grecv.at[e], s_g.at[e], r_g.at[e], snd_dev(e)))
            back[-1].start()
    for c in back:
        c.wait_recv()
    share = grecv[0, cap:, :]
    for e in range(1, n_s):
        share = share + grecv[e, cap:, :]
    trecv[0] = share
    last = [remote(trecv.at[0], trecv.at[f], s_t.at[f], r_t.at[f], map_dev(f)) for f in range(1, n_m)]
    for c in last:
        c.start()

    for e in range(n_s):
        vecs[0, pl.ds(e * cap, cap), :] = grecv[e, 0:cap, :]
    hi, mid, low = split3(vecs[0])
    placed = (dot(sel, hi, ((0,), (0,))) + dot(sel, mid, ((0,), (0,)))) + dot(sel, low, ((0,), (0,)))
    fg[...] = placed
    for t in range(tiles):
        grad_out[:, pl.ds(t * tile, tile)] = fg[pl.ds(slots * t, slots), :]

    for c in last:
        c.wait_recv()
    share = trecv[lax.rem(mm + n_m, n_m)]
    for a in range(1, n_m):
        share = share + trecv[lax.rem(mm - a + n_m, n_m)]
    class_out[0:1, :] = share[0:1, :nclass] + q_v[...] / PRIOR_VAR
    class_out[1:, :] = share[1:, :nclass] + r_v[...] / PRIOR_VAR
    prior = jnp.sum(q_v[...] * q_v[...], keepdims=True) + jnp.sum(r_v[...] * r_v[...], keepdims=True)
    cost_out[...] = share[0:1, nclass : nclass + 1] + 0.5 * prior / PRIOR_VAR

    for c in req + obs + rep + swap + back + last:
        c.wait_send()


def shards(
    n_s,
    n_m,
    sensitivity_blocks,
    block_placement_table,
    needed_tile_lists,
    location_category,
    ground_warmth_celsius,
    wetness_factor,
    carbon_reservoirs,
    category_sensitivity_effect,
    reservoir_decay_effect,
    measured_anomaly,
    retrieval_precision,
):
    nb, tile, _ = sensitivity_blocks.shape
    slots, cells = ground_warmth_celsius.shape
    pools, nclass = reservoir_decay_effect.shape
    tiles = cells // tile
    cap = needed_tile_lists.shape[1]
    nreq = n_s * cap
    rows = measured_anomaly.shape[0]
    allrows = rows * n_m
    hbm = pl.BlockSpec(memory_space=pl.ANY)
    vmem = pl.BlockSpec(memory_space=pltpu.VMEM)
    smem = pl.BlockSpec(memory_space=pltpu.SMEM)
    sem = pltpu.SemaphoreType.DMA
    blocks = nb * tile
    model, grad, classes, cost = pl.pallas_call(
        functools.partial(kernel, n_s, n_m),
        out_shape=(
            jax.ShapeDtypeStruct((rows, tile), F32),
            jax.ShapeDtypeStruct((slots, cells), F32),
            jax.ShapeDtypeStruct((1 + pools, nclass), F32),
            jax.ShapeDtypeStruct((1, 1), F32),
        ),
        in_specs=[hbm, vmem, smem, hbm, hbm, hbm, hbm, smem, smem, vmem, vmem, hbm, hbm],
        out_specs=(vmem, vmem, vmem, vmem),
        scratch_shapes=[
            pltpu.VMEM((blocks, tile), BF16),
            pltpu.VMEM((tiles, tile), jnp.int32),
            pltpu.VMEM((slots, cells), F32),
            pltpu.VMEM((slots, cells), F32),
            pltpu.VMEM((pools, cells), F32),
            pltpu.VMEM((tiles * slots, tile), F32),
            pltpu.VMEM((tiles * slots, tile), F32),
            pltpu.VMEM((tiles * 4, tile), F32),
            pltpu.VMEM((n_s, cap, tile), jnp.int32),
            pltpu.VMEM((n_s, cap, tile), jnp.int32),
            pltpu.VMEM((n_s, 2 * cap, tile), F32),
            pltpu.VMEM((n_s, 2 * cap, tile), F32),
            pltpu.VMEM((n_m, 2, rows, tile), F32),
            pltpu.VMEM((n_m, allrows, tile), F32),
            pltpu.VMEM((n_s, cap + 1 + pools, tile), F32),
            pltpu.VMEM((n_s, cap + 1 + pools, tile), F32),
            pltpu.VMEM((1 + pools, tile), F32),
            pltpu.VMEM((n_m, 1 + pools, tile), F32),
            pltpu.VMEM((2, nreq, tile), jnp.int32),
            pltpu.VMEM((2, nreq, tile), F32),
            pltpu.VMEM((nb, tile), F32),
            pltpu.VMEM((nb, tile), F32),
            pltpu.VMEM((allrows, tile), F32),
            pltpu.VMEM((tiles * slots, tile), F32),
            pltpu.VMEM(((1 + pools) * nclass, tile), F32),
            sem((7,)),
            sem((n_s,)),
            sem((n_s,)),
            sem((n_s,)),
            sem((n_s,)),
            sem((n_m, 2)),
            sem((n_m, 2)),
            sem((n_m,)),
            sem((n_m,)),
            sem((n_s,)),
            sem((n_s,)),
            sem((n_m,)),
            sem((n_m,)),
        ],
        compiler_params=pltpu.CompilerParams(
            collective_id=0, has_side_effects=True, vmem_limit_bytes=24 * 1024 * 1024
        ),
        cost_estimate=pl.CostEstimate(
            flops=2 * blocks * tile * (allrows + nreq), bytes_accessed=2 * blocks * tile, transcendentals=4 * nreq * tile
        ),
        name="inversion",
    )(
        sensitivity_blocks.reshape(blocks, tile),
        block_placement_table,
        needed_tile_lists,
        location_category.reshape(tiles, tile),
        ground_warmth_celsius,
        wetness_factor,
        carbon_reservoirs,
        category_sensitivity_effect,
        reservoir_decay_effect,
        category_sensitivity_effect.reshape(1, nclass),
        reservoir_decay_effect,
        measured_anomaly,
        retrieval_precision,
    )
    return model, grad, classes, cost.reshape(())


def solution(mesh):
    in_specs = (
        P(("snd", "map"), None, None),
        P(None, ("snd", "map")),
        P(("snd", "map"), None),
        P("map"),
        P("snd", "map"),
        P("snd", "map"),
        P(None, "map"),
        P(),
        P(),
        P(("snd", "map"), None),
        P(("snd", "map"), None),
    )
    out_specs = (P(("snd", "map"), None), P("snd", "map"), P(), P())
    return jax.shard_map(
        functools.partial(shards, mesh.shape["snd"], mesh.shape["map"]),
        mesh=mesh,
        in_specs=in_specs,
        out_specs=out_specs,
        check_vma=False,
    )
```

time: 209 us -> 46 us (0.22)
  waiting for transfers between devices: 87.9 us -> 0 us
  blocking collectives: 77.3 us -> 0 us
  Pallas kernels: 0 us -> 31.6 us
  between operations: 18.6 us -> 2.41 us
  matrix products: 11.4 us -> 0 us
  other arithmetic: 8.75 us -> 0 us
  local copies, waits for them, and re-layouts: 3.86 us -> 11.5 us
    unnamed x3 -> x0, waiting for transfers between devices: 68.2 us -> none
    psum x1 -> x0, blocking collectives: 39.6 us -> none  [shards(): class_total = lax.psum(class_part, ('snd', 'map'))]
    all_gather x2 -> x0, blocking collectives: 37.7 us -> none  [the longest x1 32.5 us: shards(): everything = lax.all_gather(flux_low, 'snd', axis=0, tiled=True)]
    pallas_call x0 -> x1, Pallas kernels: none -> 31.6 us  [shards(): pl.pallas_call(functools.partial(kernel, n_s, n_m), out_shape=(jax.ShapeD...]
    reduce_scatter x1 -> x0, waiting for transfers between devices: 19.7 us -> none  [shards(): lax.psum_scatter(partial_rows, 'map', scatter_dimension=0, tiled=True)]
    dot_general x6 -> x0, matrix products: 11.4 us -> none  [the longest x1 4.43 us: shards(): jnp.einsum('bij,bj->bi', sensitivity_blocks, vectors, preferred_element_t...]
    unnamed x15 -> x24, local copies, waits for them, and re-layouts: 0.64 us -> 11.5 us
    reduce_sum x4 -> x0, other arithmetic: 4.23 us -> none  [the longest x1 1.73 us: shards(): jnp.sum(flux_grad * device_number[0], axis=0)]
  transfers between devices with their start and end apart: 2 -> 0, of which waited for: 2 -> 0; matrix products, arithmetic and copies ran while one was open for 1% -> 0% of each run, Pallas kernels for 0% -> 0%
where the time goes in v1:
time: 46 us; the launch traced here: 45.5 us
  Pallas kernels  31.6 us (69%)
  local copies, waits for them, and re-layouts  11.5 us (25%)
  between operations  2.41 us (5%)
    pallas_call x1, Pallas kernels, shards(): pl.pallas_call(functools.partial(kernel, n_s, n_m), out_shape=(jax.ShapeD...  31.6 us
    unnamed x24, local copies, waits for them, and re-layouts  11.5 us

profile of v1, /device:TPU:0, one launch (start us, length us, event | category | flops | bytes accessed | tf_op | source)
XLA Modules:
  0.0 45.5 jit_solution(9395614443445144047)
XLA Ops:
  0.6 0.8 %copy.15.lists = s32[8,4]{1,0:T(8,128)S(1)} copy(s32[8,4]{0,1:T(4,128)} %param.13) | data formatting | bytes 256 | tf_op args[2]
  1.4 0.0 copy-start
  1.4 2.2 %copy-done = bf16[128,128,128]{2,1,0:T(8,128)(2,1)S(1)} copy-done((bf16[128,128,128]{2,1,0:T(8,128)(2,1)S(1)}, bf16[128,128,128]{2,1,0:T(8,128)(2,1)}, u32[]{:S(2)}) %copy-start) | copy-done | bytes 4194328
  3.6 0.0 copy-start.1
  3.6 0.9 %copy-done.1 = f32[3,8192]{1,0:T(4,128)S(1)} copy-done((f32[3,8192]{1,0:T(4,128)S(1)}, f32[3,8192]{1,0:T(4,128)}, u32[]{:S(2)}) %copy-start.1) | copy-done | bytes 98328
  4.5 0.0 copy-start.2
  4.5 0.8 %copy-done.2 = f32[2,8192]{1,0:T(2,128)S(1)} copy-done((f32[2,8192]{1,0:T(2,128)S(1)}, f32[2,8192]{1,0:T(2,128)}, u32[]{:S(2)}) %copy-start.2) | copy-done | bytes 65560
  5.3 0.0 copy-start.3
  5.3 0.8 %copy-done.3 = f32[2,8192]{1,0:T(2,128)S(1)} copy-done((f32[2,8192]{1,0:T(2,128)S(1)}, f32[2,8192]{1,0:T(2,128)}, u32[]{:S(2)}) %copy-start.3) | copy-done | bytes 65560
  6.2 0.0 copy-start.4
  6.2 0.8 %copy-done.4 = s32[8192]{0:T(1024)S(1)} copy-done((s32[8192]{0:T(1024)S(1)}, s32[8192]{0:T(1024)}, u32[]{:S(2)}) %copy-start.4) | copy-done | bytes 32792
  6.9 0.0 copy-start.5
  6.9 0.7 %copy-done.5 = f32[16,128]{1,0:T(8,128)S(1)} copy-done((f32[16,128]{1,0:T(8,128)S(1)}, f32[16,128]{1,0:T(8,128)}, u32[]{:S(2)}) %copy-start.5) | copy-done | bytes 8216
  7.6 0.0 copy-start.6
  7.6 0.7 %copy-done.6 = f32[16,128]{1,0:T(8,128)S(1)} copy-done((f32[16,128]{1,0:T(8,128)S(1)}, f32[16,128]{1,0:T(8,128)}, u32[]{:S(2)}) %copy-start.6) | copy-done | bytes 8216
  8.3 0.0 copy-start.7
  8.3 0.7 %copy-done.7 = f32[3,16]{1,0:T(4,128)S(1)} copy-done((f32[3,16]{1,0:T(4,128)S(1)}, f32[3,16]{1,0:T(4,128)}, u32[]{:S(2)}) %copy-start.7) | copy-done | bytes 216
  9.0 0.0 copy-start.8
  9.0 0.7 %copy-done.8 = s32[3,128]{1,0:T(4,128)S(1)} copy-done((s32[3,128]{1,0:T(4,128)S(1)}, s32[3,128]{1,0:T(4,128)}, u32[]{:S(2)}) %copy-start.8) | copy-done | bytes 1560
  9.7 0.0 copy-start.9
  9.7 0.7 %copy-done.9 = f32[16]{0:T(128)S(1)} copy-done((f32[16]{0:T(128)S(1)}, f32[16]{0:T(128)}, u32[]{:S(2)}) %copy-start.9) | copy-done | bytes 88
  10.3 31.6 %inversion.1 = (f32[16,128]{1,0:T(8,128)S(1)}, f32[2,8192]{1,0:T(2,128)S(1)}, f32[4,16]{1,0:T(4,128)S(1)}, f32[1,1]{1,0:T(1,128)}) custom-call(bf16[16384,128]{1,0:T(8,128)(2,1)S(1)} %bitcast.4, s32[3,128]{1,0:T(4,128)S(1)} %copy-done.8, s32[8,4]{1,0:T(8,128)S(1)} %copy.15.lists, s32[64,128]{1,0:T(8,128)S(1)} %bitcast.5, f32[2,8192]{1,0:T(2,128)S(1)} %copy-done.2, ...), custom_call_target="tpu_custom_call" | custom-call | flops 402653184 | bytes 4194304 | tf_op jit(solution)/shard_map/inversion/pallas_call | solution.py:334
  41.9 0.6 %copy.20 = f32[16,128]{1,0:T(8,128)} copy(f32[16,128]{1,0:T(8,128)S(1)} %get-tuple-element.16) | data formatting | bytes 16384
  42.5 0.6 %copy.21 = f32[2,8192]{1,0:T(2,128)} copy(f32[2,8192]{1,0:T(2,128)S(1)} %get-tuple-element.17) | data formatting | bytes 131072
  43.1 0.6 %copy.22 = f32[4,16]{1,0:T(4,128)} copy(f32[4,16]{1,0:T(4,128)S(1)} %get-tuple-element.18) | data formatting | bytes 512
Async XLA Ops:
  1.4 2.2 %copy-start = (bf16[128,128,128]{2,1,0:T(8,128)(2,1)S(1)}, bf16[128,128,128]{2,1,0:T(8,128)(2,1)}, u32[]{:S(2)}) copy-start(bf16[128,128,128]{2,1,0:T(8,128)(2,1)} %param.11) | copy-start | bytes 12582916
  3.6 0.9 %copy-start.1 = (f32[3,8192]{1,0:T(4,128)S(1)}, f32[3,8192]{1,0:T(4,128)}, u32[]{:S(2)}) copy-start(f32[3,8192]{1,0:T(4,128)} %carb_hbm.1) | copy-start | bytes 294916
  4.5 0.8 %copy-start.2 = (f32[2,8192]{1,0:T(2,128)S(1)}, f32[2,8192]{1,0:T(2,128)}, u32[]{:S(2)}) copy-start(f32[2,8192]{1,0:T(2,128)} %warm_hbm.1) | copy-start | bytes 196612
  5.3 0.8 %copy-start.3 = (f32[2,8192]{1,0:T(2,128)S(1)}, f32[2,8192]{1,0:T(2,128)}, u32[]{:S(2)}) copy-start(f32[2,8192]{1,0:T(2,128)} %wet_hbm.1) | copy-start | bytes 196612
  6.2 0.8 %copy-start.4 = (s32[8192]{0:T(1024)S(1)}, s32[8192]{0:T(1024)}, u32[]{:S(2)}) copy-start(s32[8192]{0:T(1024)} %param.14) | copy-start | bytes 98308
  6.9 0.7 %copy-start.5 = (f32[16,128]{1,0:T(8,128)S(1)}, f32[16,128]{1,0:T(8,128)}, u32[]{:S(2)}) copy-start(f32[16,128]{1,0:T(8,128)} %meas_hbm.1) | copy-start | bytes 24580
  7.6 0.7 %copy-start.6 = (f32[16,128]{1,0:T(8,128)S(1)}, f32[16,128]{1,0:T(8,128)}, u32[]{:S(2)}) copy-start(f32[16,128]{1,0:T(8,128)} %prec_hbm.1) | copy-start | bytes 24580
  8.3 0.7 %copy-start.7 = (f32[3,16]{1,0:T(4,128)S(1)}, f32[3,16]{1,0:T(4,128)}, u32[]{:S(2)}) copy-start(f32[3,16]{1,0:T(4,128)} %r_v.1) | copy-start | bytes 580
  9.0 0.7 %copy-start.8 = (s32[3,128]{1,0:T(4,128)S(1)}, s32[3,128]{1,0:T(4,128)}, u32[]{:S(2)}) copy-start(s32[3,128]{1,0:T(4,128)} %table.1) | copy-start | bytes 4612
  9.7 0.7 %copy-start.9 = (f32[16]{0:T(128)S(1)}, f32[16]{0:T(128)}, u32[]{:S(2)}) copy-start(f32[16]{0:T(128)} %q_s.1) | copy-start | bytes 196

commit v2 on v1

--- a/solution.py
+++ b/solution.py
@@ -11,7 +11,7 @@
 LOG_BASE_Q = 0.6931471805599453
 PRIOR_VAR = 0.09
 RATES = (0.6, 0.25, 0.1)
-CHUNK = 8
+CHUNK = 32
 F32 = jnp.float32
 BF16 = jnp.bfloat16
 
@@ -42,14 +42,14 @@
 
 
 def kernel(
-    n_s, n_m, sens_hbm, table, lists, cat_hbm, warm_hbm, wet_hbm, carb_hbm, q_s, r_s, q_v, r_v, meas_hbm, prec_hbm,
-    model_out, grad_out, class_out, cost_out,
-    sens, cat, warm_in, wet_in, carb_in, warm, wet, carb,
+    n_s, n_m, sens_hbm, table_hbm, lists, cat_hbm, warm_hbm, wet_hbm, carb_hbm, q_s, r_s, q_hbm, r_hbm, meas_hbm,
+    prec_hbm, model_hbm, grad_hbm, class_hbm, cost_hbm,
+    model_out, grad_out, class_out, cost_out, table, q_v, r_v, vb, sens, cat, warm_in, wet_in, carb_in, warm, wet, carb,
     req_send, req_recv, rep_send, rep_recv, mbuf, part, gsend, grecv, tsend, trecv,
     ids, vecs, tcol, rcol, model, fg, srows,
-    local_sem, s_req, r_req, s_rep, r_rep, s_m, r_m, s_p, r_p, s_g, r_g, s_t, r_t,
+    local_sem, out_sem, s_req, r_req, s_rep, r_rep, s_m, r_m, s_p, r_p, s_g, r_g, s_t, r_t,
 ):
-    cap = lists.shape[1]
+    cap = lists.shape[0]
     nreq = n_s * cap
     slots = warm_hbm.shape[0]
     tiles = cat.shape[0]
@@ -81,10 +81,13 @@
             [
                 (warm_hbm, warm_in),
                 (wet_hbm, wet_in),
+                (table_hbm, table),
                 (carb_hbm, carb_in),
                 (cat_hbm, cat),
                 (meas_hbm, mbuf.at[0, 0]),
                 (prec_hbm, mbuf.at[0, 1]),
+                (q_hbm, q_v),
+                (r_hbm, r_v),
                 (sens_hbm, sens),
             ]
         )
@@ -99,7 +102,7 @@
         spot = jnp.full((cap, tile), -1, jnp.int32)
         tile_id = jnp.full((cap, tile), -1, jnp.int32)
         for k in range(cap):
-            asked = lists[owner, k]
+            asked = lists[k, owner]
             t = lax.rem(asked, tiles)
             here = row_in == k
             whole_id = jnp.where(here, jnp.where(asked < 0, -1, owner * (slots * tiles) + asked), whole_id)
@@ -125,16 +128,42 @@
         c.start()
 
     carb[...] = jnp.zeros_like(carb)
-    for load in loads[:4]:
+    for load in loads[:3]:
         load.wait()
     for t in range(tiles):
         lanes = pl.ds(t * tile, tile)
         warm[pl.ds(slots * t, slots), :] = warm_in[:, lanes]
         wet[pl.ds(slots * t, slots), :] = wet_in[:, lanes]
-        carb[pl.ds(4 * t, pools), :] = carb_in[:, lanes]
-    warm_parts = split3(warm[...])
-    wet_parts = split3(wet[...])
-
+    observed = jnp.concatenate(split3(warm[...]) + split3(wet[...]), axis=1)
+
+    block_row = table[0:1, :]
+    block_id = table[2:3, :] * tiles + table[1:2, :]
+    asked_hot = onehot(ids[0][:, :nb] == block_id)
+    row_hot = onehot(iota((allrows, nb), 0) == block_row)
+    tcol[...] = dot(asked_hot, iota((nreq, tile), 0).astype(F32).astype(BF16), ((0,), (0,)))
+    rcol[...] = dot(row_hot, iota((allrows, tile), 0).astype(F32).astype(BF16), ((0,), (0,)))
+
+    for c in req:
+        c.wait_recv()
+    for e in range(n_s):
+        ids[0, pl.ds(e * cap, cap), :] = req_recv[e]
+    sel = onehot(ids[0] == iota((nreq, tile), 1))
+    every = dot(sel, observed, ((1,), (0,)))
+    cut = [every[:, i * tile : (i + 1) * tile] for i in range(6)]
+    out_warm = (cut[0] + cut[1]) + cut[2]
+    out_wet = (cut[3] + cut[4]) + cut[5]
+    rep = []
+    for e in range(n_s):
+        to = rep_recv if e == 0 else rep_send
+        to[e, 0:cap, :] = out_warm[e * cap : (e + 1) * cap]
+        to[e, cap : 2 * cap, :] = out_wet[e * cap : (e + 1) * cap]
+        if e:
+            rep.append(remote(rep_send.at[e], rep_recv.at[e], s_rep.at[e], r_rep.at[e], snd_dev(-e)))
+            rep[-1].start()
+    for load in loads[3:5]:
+        load.wait()
+    for t in range(tiles):
+        carb[pl.ds(4 * t, pools), :] = carb_in[:, pl.ds(t * tile, tile)]
     tile_id = ids[1]
     cls = dot(onehot(tile_id[:, :tiles] == iota((nreq, tiles), 1)), cat[...].astype(F32).astype(BF16), ((1,), (0,)))
     cls = cls.astype(jnp.int32)
@@ -153,30 +182,6 @@
         carbon = pick(onehot(wide * 4 + p == wide_at), carb[...])
         held.append(RATES[p] * jnp.exp(effects[p]) * carbon)
 
-    block_row = table[0:1, :]
-    block_id = table[2:3, :] * tiles + table[1:2, :]
-    asked_hot = onehot(ids[0][:, :nb] == block_id)
-    row_hot = onehot(iota((allrows, nb), 0) == block_row)
-    tcol[...] = dot(asked_hot, iota((nreq, tile), 0).astype(F32).astype(BF16), ((0,), (0,)))
-    rcol[...] = dot(row_hot, iota((allrows, tile), 0).astype(F32).astype(BF16), ((0,), (0,)))
-
-    for c in req:
-        c.wait_recv()
-    for e in range(n_s):
-        ids[0, pl.ds(e * cap, cap), :] = req_recv[e]
-    sel = onehot(ids[0] == iota((nreq, tile), 1))
-    every = dot(sel, jnp.concatenate(list(warm_parts) + list(wet_parts), axis=1), ((1,), (0,)))
-    cut = [every[:, i * tile : (i + 1) * tile] for i in range(6)]
-    out_warm = (cut[0] + cut[1]) + cut[2]
-    out_wet = (cut[3] + cut[4]) + cut[5]
-    rep = []
-    for e in range(n_s):
-        to = rep_recv if e == 0 else rep_send
-        to[e, 0:cap, :] = out_warm[e * cap : (e + 1) * cap]
-        to[e, cap : 2 * cap, :] = out_wet[e * cap : (e + 1) * cap]
-        if e:
-            rep.append(remote(rep_send.at[e], rep_recv.at[e], s_rep.at[e], r_rep.at[e], snd_dev(-e)))
-            rep[-1].start()
     for c in rep:
         c.wait_recv()
     for e in range(n_s):
@@ -192,9 +197,8 @@
     tcol_hot = onehot(tcol[:, :nreq] == iota((nb, nreq), 1).astype(F32))
     vecs_b = dot(tcol_hot, flux_low, ((1,), (0,)))
     model_at = iota((allrows, tile), 0).astype(F32)
-    vb = fg
     vb[...] = vecs_b
-    loads[6].wait()
+    loads[9].wait()
 
     def forward(step, acc):
         at = pl.multiple_of(step * CHUNK, CHUNK)
@@ -211,7 +215,7 @@
     swap = [remote(part.at[0], part.at[f], s_p.at[f], r_p.at[f], map_dev(f)) for f in range(1, n_m)]
     for c in swap:
         c.start()
-    for c in loads[4:6]:
+    for c in loads[5:9]:
         c.wait()
     for c in obs:
         c.wait_recv()
@@ -233,6 +237,13 @@
     weighted = (diff * prec).astype(BF16)
     own = model[pl.ds(pl.multiple_of(mm * rows, rows), rows), :]
     model_out[...] = own
+    outs = [
+        pltpu.make_async_copy(src, dst, out_sem.at[i])
+        for i, (src, dst) in enumerate(
+            [(model_out, model_hbm), (grad_out, grad_hbm), (class_out, class_hbm), (cost_out, cost_hbm)]
+        )
+    ]
+    outs[0].start()
     own_diff = own - mbuf[0, 0]
     misfit = 0.5 * jnp.sum(mbuf[0, 1] * own_diff * own_diff, keepdims=True)
 
@@ -288,6 +299,7 @@
     fg[...] = placed
     for t in range(tiles):
         grad_out[:, pl.ds(t * tile, tile)] = fg[pl.ds(slots * t, slots), :]
+    outs[1].start()
 
     for c in last:
         c.wait_recv()
@@ -299,8 +311,21 @@
     prior = jnp.sum(q_v[...] * q_v[...], keepdims=True) + jnp.sum(r_v[...] * r_v[...], keepdims=True)
     cost_out[...] = share[0:1, nclass : nclass + 1] + 0.5 * prior / PRIOR_VAR
 
+    outs[2].start()
+    outs[3].start()
     for c in req + obs + rep + swap + back + last:
         c.wait_send()
+    for c in outs:
+        c.wait()
+
+
+def hand_over(*refs):
+    n = len(refs) // 2
+    copies = [pltpu.make_async_copy(refs[i], refs[n + i], refs[2 * n].at[i]) for i in range(n)]
+    for c in copies:
+        c.start()
+    for c in copies:
+        c.wait()
 
 
 def shards(
@@ -327,21 +352,29 @@
     rows = measured_anomaly.shape[0]
     allrows = rows * n_m
     hbm = pl.BlockSpec(memory_space=pl.ANY)
-    vmem = pl.BlockSpec(memory_space=pltpu.VMEM)
+    results = (
+        jax.ShapeDtypeStruct((rows, tile), F32),
+        jax.ShapeDtypeStruct((slots, cells), F32),
+        jax.ShapeDtypeStruct((1 + pools, nclass), F32),
+        jax.ShapeDtypeStruct((1, 1), F32),
+    )
     smem = pl.BlockSpec(memory_space=pltpu.SMEM)
     sem = pltpu.SemaphoreType.DMA
     blocks = nb * tile
-    model, grad, classes, cost = pl.pallas_call(
+    outs = pl.pallas_call(
         functools.partial(kernel, n_s, n_m),
-        out_shape=(
-            jax.ShapeDtypeStruct((rows, tile), F32),
-            jax.ShapeDtypeStruct((slots, cells), F32),
-            jax.ShapeDtypeStruct((1 + pools, nclass), F32),
-            jax.ShapeDtypeStruct((1, 1), F32),
-        ),
-        in_specs=[hbm, vmem, smem, hbm, hbm, hbm, hbm, smem, smem, vmem, vmem, hbm, hbm],
-        out_specs=(vmem, vmem, vmem, vmem),
+        out_shape=results,
+        in_specs=[hbm, hbm, smem, hbm, hbm, hbm, hbm, smem, smem, hbm, hbm, hbm, hbm],
+        out_specs=(hbm,) * 4,
         scratch_shapes=[
+            pltpu.VMEM((rows, tile), F32),
+            pltpu.VMEM((slots, cells), F32),
+            pltpu.VMEM((1 + pools, nclass), F32),
+            pltpu.VMEM((1, 1), F32),
+            pltpu.VMEM((3, nb), jnp.int32),
+            pltpu.VMEM((1, nclass), F32),
+            pltpu.VMEM((pools, nclass), F32),
+            pltpu.VMEM((nb, tile), F32),
             pltpu.VMEM((blocks, tile), BF16),
             pltpu.VMEM((tiles, tile), jnp.int32),
             pltpu.VMEM((slots, cells), F32),
@@ -367,7 +400,8 @@
             pltpu.VMEM((allrows, tile), F32),
             pltpu.VMEM((tiles * slots, tile), F32),
             pltpu.VMEM(((1 + pools) * nclass, tile), F32),
-            sem((7,)),
+            sem((10,)),
+            sem((4,)),
             sem((n_s,)),
             sem((n_s,)),
             sem((n_s,)),
@@ -381,9 +415,7 @@
             sem((n_m,)),
             sem((n_m,)),
         ],
-        compiler_params=pltpu.CompilerParams(
-            collective_id=0, has_side_effects=True, vmem_limit_bytes=24 * 1024 * 1024
-        ),
+        compiler_params=pltpu.CompilerParams(collective_id=0, has_side_effects=True),
         cost_estimate=pl.CostEstimate(
             flops=2 * blocks * tile * (allrows + nreq), bytes_accessed=2 * blocks * tile, transcendentals=4 * nreq * tile
         ),
@@ -391,7 +423,7 @@
     )(
         sensitivity_blocks.reshape(blocks, tile),
         block_placement_table,
-        needed_tile_lists,
+        needed_tile_lists.T,
         location_category.reshape(tiles, tile),
         ground_warmth_celsius,
         wetness_factor,
@@ -403,6 +435,14 @@
         measured_anomaly,
         retrieval_precision,
     )
+    model, grad, classes, cost = pl.pallas_call(
+        hand_over,
+        out_shape=results,
+        in_specs=[hbm] * 4,
+        out_specs=(hbm,) * 4,
+        scratch_shapes=[sem((4,))],
+        name="results",
+    )(*outs)
     return model, grad, classes, cost.reshape(())
 
 

time: 46 us -> 33.4 us (0.73)
  local copies, waits for them, and re-layouts: 11.5 us -> 0 us
  between operations: 2.41 us -> 0.64 us
  Pallas kernels: 31.6 us -> 32.6 us
    unnamed x24 -> x0, local copies, waits for them, and re-layouts: 11.5 us -> none
    pallas_call x1 -> x2, Pallas kernels: 31.6 us -> 32.6 us  [the longest x1 28.6 us: shards(): pl.pallas_call(functools.partial(kernel, n_s, n_m), out_shape=results, in...]
where the time goes in v2:
time: 33.4 us; the launch traced here: 33.2 us
  Pallas kernels  32.6 us (98%)
  between operations  0.64 us (2%)
    pallas_call x1, Pallas kernels, shards(): pl.pallas_call(functools.partial(kernel, n_s, n_m), out_shape=results, in...  28.6 us
    pallas_call x1, Pallas kernels, shards(): pl.pallas_call(hand_over, out_shape=results, in_specs=[hbm] * 4, out_spec...  3.99 us

profile of v2, /device:TPU:0, one launch (start us, length us, event | category | flops | bytes accessed | tf_op | source)
XLA Modules:
  0.0 33.2 jit_solution(9124551422704752530)
XLA Ops:
  0.6 28.6 %inversion.1 = (f32[16,128]{1,0:T(8,128)}, f32[2,8192]{1,0:T(2,128)}, f32[4,16]{1,0:T(4,128)}, f32[1,1]{1,0:T(1,128)}) custom-call(bf16[16384,128]{1,0:T(8,128)(2,1)} %bitcast.5, s32[3,128]{1,0:T(4,128)} %table_hbm.1, s32[4,8]{1,0:T(4,128)} %bitcast.7, s32[64,128]{1,0:T(8,128)} %bitcast.6, f32[2,8192]{1,0:T(2,128)} %warm_hbm.1, f32[2,8192]{1,0:T(2,128)} %wet_hbm.1, ...), custom_call_target="tpu_custom_call" | custom-call | flops 402653184 | bytes 4194304 | tf_op jit(solution)/shard_map/inversion/pallas_call | solution.py:364
  29.3 4.0 %results.1 = (f32[16,128]{1,0:T(8,128)}, f32[2,8192]{1,0:T(2,128)}, f32[4,16]{1,0:T(4,128)}, f32[1,1]{1,0:T(1,128)}) custom-call(f32[16,128]{1,0:T(8,128)} %get-tuple-element.12.refs_0_, f32[2,8192]{1,0:T(2,128)} %get-tuple-element.13.refs_1_, f32[4,16]{1,0:T(4,128)} %get-tuple-element.14.refs_2_, f32[1,1]{1,0:T(1,128)} %get-tuple-element.15.refs_3_), custom_call_target="tpu_custom_call" | custom-call | tf_op jit(solution)/shard_map/results/pallas_call | solution.py:438

commit v3 on v2

--- a/solution.py
+++ b/solution.py
@@ -11,7 +11,7 @@
 LOG_BASE_Q = 0.6931471805599453
 PRIOR_VAR = 0.09
 RATES = (0.6, 0.25, 0.1)
-CHUNK = 32
+CHUNK = 16
 F32 = jnp.float32
 BF16 = jnp.bfloat16
 
@@ -182,6 +182,7 @@
         carbon = pick(onehot(wide * 4 + p == wide_at), carb[...])
         held.append(RATES[p] * jnp.exp(effects[p]) * carbon)
 
+    tcol_hot = onehot(tcol[:, :nreq] == iota((nb, nreq), 1).astype(F32))
     for c in rep:
         c.wait_recv()
     for e in range(n_s):
@@ -194,23 +195,19 @@
     flux = pieces[0] + pieces[1] + pieces[2]
     flux_low = flux.astype(BF16)
 
-    tcol_hot = onehot(tcol[:, :nreq] == iota((nb, nreq), 1).astype(F32))
     vecs_b = dot(tcol_hot, flux_low, ((1,), (0,)))
     model_at = iota((allrows, tile), 0).astype(F32)
     vb[...] = vecs_b
     loads[9].wait()
 
-    def forward(step, acc):
-        at = pl.multiple_of(step * CHUNK, CHUNK)
-        v = vb[pl.ds(at, CHUNK), :]
-        r = rcol[pl.ds(at, CHUNK), :]
-        left = [jnp.where(model_at == r[u : u + 1], v[u : u + 1], 0.0).astype(BF16) for u in range(CHUNK)]
-        right = [
-            sens[pl.ds(pl.multiple_of((step * CHUNK + u) * tile, tile), tile), :] for u in range(CHUNK)
+    partial = jnp.zeros((allrows, tile), F32)
+    for at in range(0, nb, CHUNK):
+        left = [
+            jnp.where(model_at == rcol[b : b + 1, :], vb[b : b + 1, :], 0.0).astype(BF16) for b in range(at, at + CHUNK)
         ]
-        return acc + dot(jnp.concatenate(left, axis=1), jnp.concatenate(right, axis=1), ((1,), (1,)))
-
-    part[0] = lax.fori_loop(0, nb // CHUNK, forward, jnp.zeros((allrows, tile), F32))
+        right = [sens[b * tile : (b + 1) * tile, :] for b in range(at, at + CHUNK)]
+        partial += dot(jnp.concatenate(left, axis=1), jnp.concatenate(right, axis=1), ((1,), (1,)))
+    part[0] = partial
 
     swap = [remote(part.at[0], part.at[f], s_p.at[f], r_p.at[f], map_dev(f)) for f in range(1, n_m)]
     for c in swap:
@@ -250,15 +247,12 @@
     vb[...] = dot(rcol_hot, weighted, ((1,), (0,)))
     asked_at = iota((nreq, tile), 0).astype(F32)
 
-    def backward(step, acc):
-        at = pl.multiple_of(step * CHUNK, CHUNK)
-        v = vb[pl.ds(at, CHUNK), :]
-        r = tcol[pl.ds(at, CHUNK), :]
-        left = [jnp.where(asked_at == r[u : u + 1], v[u : u + 1], 0.0).astype(BF16) for u in range(CHUNK)]
-        right = sens[pl.ds(pl.multiple_of(step * CHUNK * tile, CHUNK * tile), CHUNK * tile), :]
-        return acc + dot(jnp.concatenate(left, axis=1), right, ((1,), (0,)))
-
-    grads = lax.fori_loop(0, nb // CHUNK, backward, jnp.zeros((nreq, tile), F32))
+    grads = jnp.zeros((nreq, tile), F32)
+    for at in range(0, nb, CHUNK):
+        left = [
+            jnp.where(asked_at == tcol[b : b + 1, :], vb[b : b + 1, :], 0.0).astype(BF16) for b in range(at, at + CHUNK)
+        ]
+        grads += dot(jnp.concatenate(left, axis=1), sens[at * tile : (at + CHUNK) * tile, :], ((1,), (0,)))
 
     terms = [grads * flux * tau] + [grads * piece for piece in pieces]
     for c in range(nclass):
@@ -320,12 +314,17 @@
 
 
 def hand_over(*refs):
-    n = len(refs) // 2
-    copies = [pltpu.make_async_copy(refs[i], refs[n + i], refs[2 * n].at[i]) for i in range(n)]
-    for c in copies:
+    n = len(refs) // 3
+    given, results, held, (sem_in, sem_out) = refs[:n], refs[n : 2 * n], refs[2 * n : 3 * n], refs[3 * n :]
+    fetch = [pltpu.make_async_copy(given[i], held[i], sem_in.at[i]) for i in range(n)]
+    write = [pltpu.make_async_copy(held[i], results[i], sem_out.at[i]) for i in range(n)]
+    for c in fetch:
         c.start()
-    for c in copies:
+    for c, w in zip(fetch, write):
         c.wait()
+        w.start()
+    for w in write:
+        w.wait()
 
 
 def shards(
@@ -440,7 +439,7 @@
         out_shape=results,
         in_specs=[hbm] * 4,
         out_specs=(hbm,) * 4,
-        scratch_shapes=[sem((4,))],
+        scratch_shapes=[pltpu.VMEM(r.shape, F32) for r in results] + [sem((4,)), sem((4,))],
         name="results",
     )(*outs)
     return model, grad, classes, cost.reshape(())

time: 33.4 us -> 31.6 us (0.946)
  Pallas kernels: 32.6 us -> 30.7 us
    pallas_call x1, Pallas kernels: 3.99 us -> 2.12 us  [shards(): pl.pallas_call(hand_over, out_shape=results, in_specs=[hbm] * 4, out_spec...]
where the time goes in v3:
time: 31.6 us; the launch traced here: 31.3 us
  Pallas kernels  30.7 us (97%)
  between operations  0.64 us (2%)
    pallas_call x1, Pallas kernels, shards(): pl.pallas_call(functools.partial(kernel, n_s, n_m), out_shape=results, in...  28.6 us
    pallas_call x1, Pallas kernels, shards(): pl.pallas_call(hand_over, out_shape=results, in_specs=[hbm] * 4, out_spec...  2.12 us

profile of v3, /device:TPU:0, one launch (start us, length us, event | category | flops | bytes accessed | tf_op | source)
XLA Modules:
  0.0 31.3 jit_solution(1190208808789378227)
XLA Ops:
  0.6 28.6 %inversion.1 = (f32[16,128]{1,0:T(8,128)}, f32[2,8192]{1,0:T(2,128)}, f32[4,16]{1,0:T(4,128)}, f32[1,1]{1,0:T(1,128)}) custom-call(bf16[16384,128]{1,0:T(8,128)(2,1)} %bitcast.5, s32[3,128]{1,0:T(4,128)} %table_hbm.1, s32[4,8]{1,0:T(4,128)} %bitcast.7, s32[64,128]{1,0:T(8,128)} %bitcast.6, f32[2,8192]{1,0:T(2,128)} %warm_hbm.1, f32[2,8192]{1,0:T(2,128)} %wet_hbm.1, ...), custom_call_target="tpu_custom_call" | custom-call | flops 402653184 | bytes 4194304 | tf_op jit(solution)/shard_map/inversion/pallas_call | solution.py:363
  29.2 2.1 %results.1 = (f32[16,128]{1,0:T(8,128)}, f32[2,8192]{1,0:T(2,128)}, f32[4,16]{1,0:T(4,128)}, f32[1,1]{1,0:T(1,128)}) custom-call(f32[16,128]{1,0:T(8,128)} %get-tuple-element.12.refs_0_, f32[2,8192]{1,0:T(2,128)} %get-tuple-element.13.refs_1_, f32[4,16]{1,0:T(4,128)} %get-tuple-element.14.refs_2_, f32[1,1]{1,0:T(1,128)} %get-tuple-element.15.refs_3_), custom_call_target="tpu_custom_call" | custom-call | tf_op jit(solution)/shard_map/results/pallas_call | solution.py:437

commit v4 on v3

--- a/solution.py
+++ b/solution.py
@@ -41,13 +41,17 @@
     return lax.broadcasted_iota(jnp.int32, shape, dim)
 
 
+def is_direct(n_s, n_m):
+    return n_s * n_m <= 64
+
+
 def kernel(
     n_s, n_m, sens_hbm, table_hbm, lists, cat_hbm, warm_hbm, wet_hbm, carb_hbm, q_s, r_s, q_hbm, r_hbm, meas_hbm,
-    prec_hbm, model_hbm, grad_hbm, class_hbm, cost_hbm,
+    prec_hbm,
     model_out, grad_out, class_out, cost_out, table, q_v, r_v, vb, sens, cat, warm_in, wet_in, carb_in, warm, wet, carb,
     req_send, req_recv, rep_send, rep_recv, mbuf, part, gsend, grecv, tsend, trecv,
     ids, vecs, tcol, rcol, model, fg, srows,
-    local_sem, out_sem, s_req, r_req, s_rep, r_rep, s_m, r_m, s_p, r_p, s_g, r_g, s_t, r_t,
+    local_sem, s_req, r_req, s_rep, r_rep, s_m, r_m, s_p, r_p, s_g, r_g, s_t, r_t,
 ):
     cap = lists.shape[0]
     nreq = n_s * cap
@@ -70,10 +74,10 @@
         )
 
     barrier = pltpu.get_barrier_semaphore()
-    for e in range(1, n_s):
-        pl.semaphore_signal(barrier, inc=1, device_id=snd_dev(e), device_id_type=pl.DeviceIdType.MESH)
-    for f in range(1, n_m):
-        pl.semaphore_signal(barrier, inc=1, device_id=map_dev(f), device_id_type=pl.DeviceIdType.MESH)
+    direct = is_direct(n_s, n_m)
+    others = [(e, f) for e in range(n_s) for f in range(n_m) if e + f and (direct or e == 0 or f == 0)]
+    for e, f in others:
+        pl.semaphore_signal(barrier, inc=1, device_id=snd_dev(e) | map_dev(f), device_id_type=pl.DeviceIdType.MESH)
 
     loads = [
         pltpu.make_async_copy(src, dst, local_sem.at[i])
@@ -115,18 +119,11 @@
         ids[0, pl.ds(e * cap, cap), :] = whole_id
         ids[1, pl.ds(e * cap, cap), :] = tile_id
 
-    pl.semaphore_wait(barrier, n_s - 1 + n_m - 1)
+    pl.semaphore_wait(barrier, len(others))
 
     req = [remote(req_send.at[e], req_recv.at[e], s_req.at[e], r_req.at[e], snd_dev(e)) for e in range(1, n_s)]
     for c in req:
         c.start()
-    obs = []
-    for f in range(1, n_m):
-        obs.append(remote(meas_hbm, mbuf.at[f, 0], s_m.at[f, 0], r_m.at[f, 0], map_dev(f)))
-        obs.append(remote(prec_hbm, mbuf.at[f, 1], s_m.at[f, 1], r_m.at[f, 1], map_dev(f)))
-    for c in obs:
-        c.start()
-
     carb[...] = jnp.zeros_like(carb)
     for load in loads[:3]:
         load.wait()
@@ -160,6 +157,12 @@
         if e:
             rep.append(remote(rep_send.at[e], rep_recv.at[e], s_rep.at[e], r_rep.at[e], snd_dev(-e)))
             rep[-1].start()
+    for load in loads[5:7]:
+        load.wait()
+    obs = [remote(mbuf.at[0], mbuf.at[f], s_m.at[f], r_m.at[f], map_dev(f)) for f in range(1, n_m)]
+    for c in obs:
+        c.start()
+
     for load in loads[3:5]:
         load.wait()
     for t in range(tiles):
@@ -212,7 +215,7 @@
     swap = [remote(part.at[0], part.at[f], s_p.at[f], r_p.at[f], map_dev(f)) for f in range(1, n_m)]
     for c in swap:
         c.start()
-    for c in loads[5:9]:
+    for c in loads[7:9]:
         c.wait()
     for c in obs:
         c.wait_recv()
@@ -234,13 +237,6 @@
     weighted = (diff * prec).astype(BF16)
     own = model[pl.ds(pl.multiple_of(mm * rows, rows), rows), :]
     model_out[...] = own
-    outs = [
-        pltpu.make_async_copy(src, dst, out_sem.at[i])
-        for i, (src, dst) in enumerate(
-            [(model_out, model_hbm), (grad_out, grad_hbm), (class_out, class_hbm), (cost_out, cost_hbm)]
-        )
-    ]
-    outs[0].start()
     own_diff = own - mbuf[0, 0]
     misfit = 0.5 * jnp.sum(mbuf[0, 1] * own_diff * own_diff, keepdims=True)
 
@@ -276,15 +272,25 @@
         if e:
             back.append(remote(gsend.at[e], grecv.at[e], s_g.at[e], r_g.at[e], snd_dev(e)))
             back[-1].start()
+    if direct:
+        tsend[...] = share
+        last = [
+            remote(tsend, trecv.at[e, f], s_t.at[e, f], r_t.at[e, f], snd_dev(e) | map_dev(f))
+            for e in range(n_s)
+            for f in range(1, n_m)
+        ]
+        for c in last:
+            c.start()
     for c in back:
         c.wait_recv()
     share = grecv[0, cap:, :]
     for e in range(1, n_s):
         share = share + grecv[e, cap:, :]
-    trecv[0] = share
-    last = [remote(trecv.at[0], trecv.at[f], s_t.at[f], r_t.at[f], map_dev(f)) for f in range(1, n_m)]
-    for c in last:
-        c.start()
+    if not direct:
+        tsend[...] = share
+        last = [remote(tsend, trecv.at[0, f], s_t.at[0, f], r_t.at[0, f], map_dev(f)) for f in range(1, n_m)]
+        for c in last:
+            c.start()
 
     for e in range(n_s):
         vecs[0, pl.ds(e * cap, cap), :] = grecv[e, 0:cap, :]
@@ -293,38 +299,32 @@
     fg[...] = placed
     for t in range(tiles):
         grad_out[:, pl.ds(t * tile, tile)] = fg[pl.ds(slots * t, slots), :]
-    outs[1].start()
 
     for c in last:
         c.wait_recv()
-    share = trecv[lax.rem(mm + n_m, n_m)]
-    for a in range(1, n_m):
-        share = share + trecv[lax.rem(mm - a + n_m, n_m)]
+    for e in range(trecv.shape[0]):
+        for f in range(1, n_m):
+            share = share + trecv[e, f]
     class_out[0:1, :] = share[0:1, :nclass] + q_v[...] / PRIOR_VAR
     class_out[1:, :] = share[1:, :nclass] + r_v[...] / PRIOR_VAR
     prior = jnp.sum(q_v[...] * q_v[...], keepdims=True) + jnp.sum(r_v[...] * r_v[...], keepdims=True)
     cost_out[...] = share[0:1, nclass : nclass + 1] + 0.5 * prior / PRIOR_VAR
 
-    outs[2].start()
-    outs[3].start()
     for c in req + obs + rep + swap + back + last:
         c.wait_send()
-    for c in outs:
+
+
+def hand_over(*refs):
+    n = len(refs) // 2
+    writes = [pltpu.make_async_copy(refs[i], refs[n + i], refs[2 * n].at[i]) for i in range(n)]
+    for c in writes:
+        c.start()
+    for c in writes:
         c.wait()
 
 
-def hand_over(*refs):
-    n = len(refs) // 3
-    given, results, held, (sem_in, sem_out) = refs[:n], refs[n : 2 * n], refs[2 * n : 3 * n], refs[3 * n :]
-    fetch = [pltpu.make_async_copy(given[i], held[i], sem_in.at[i]) for i in range(n)]
-    write = [pltpu.make_async_copy(held[i], results[i], sem_out.at[i]) for i in range(n)]
-    for c in fetch:
-        c.start()
-    for c, w in zip(fetch, write):
-        c.wait()
-        w.start()
-    for w in write:
-        w.wait()
+def pinned(x):
+    return pltpu.with_memory_space_constraint(x, pltpu.HBM)
 
 
 def shards(
@@ -350,7 +350,8 @@
     nreq = n_s * cap
     rows = measured_anomaly.shape[0]
     allrows = rows * n_m
-    hbm = pl.BlockSpec(memory_space=pl.ANY)
+    hbm = pl.BlockSpec(memory_space=pltpu.HBM)
+    vmem = pl.BlockSpec(memory_space=pltpu.VMEM)
     results = (
         jax.ShapeDtypeStruct((rows, tile), F32),
         jax.ShapeDtypeStruct((slots, cells), F32),
@@ -360,16 +361,13 @@
     smem = pl.BlockSpec(memory_space=pltpu.SMEM)
     sem = pltpu.SemaphoreType.DMA
     blocks = nb * tile
+    stage = n_s if is_direct(n_s, n_m) else 1
     outs = pl.pallas_call(
         functools.partial(kernel, n_s, n_m),
         out_shape=results,
         in_specs=[hbm, hbm, smem, hbm, hbm, hbm, hbm, smem, smem, hbm, hbm, hbm, hbm],
-        out_specs=(hbm,) * 4,
+        out_specs=(vmem,) * 4,
         scratch_shapes=[
-            pltpu.VMEM((rows, tile), F32),
-            pltpu.VMEM((slots, cells), F32),
-            pltpu.VMEM((1 + pools, nclass), F32),
-            pltpu.VMEM((1, 1), F32),
             pltpu.VMEM((3, nb), jnp.int32),
             pltpu.VMEM((1, nclass), F32),
             pltpu.VMEM((pools, nclass), F32),
@@ -391,7 +389,7 @@
             pltpu.VMEM((n_s, cap + 1 + pools, tile), F32),
             pltpu.VMEM((n_s, cap + 1 + pools, tile), F32),
             pltpu.VMEM((1 + pools, tile), F32),
-            pltpu.VMEM((n_m, 1 + pools, tile), F32),
+            pltpu.VMEM((stage, n_m, 1 + pools, tile), F32),
             pltpu.VMEM((2, nreq, tile), jnp.int32),
             pltpu.VMEM((2, nreq, tile), F32),
             pltpu.VMEM((nb, tile), F32),
@@ -400,46 +398,47 @@
             pltpu.VMEM((tiles * slots, tile), F32),
             pltpu.VMEM(((1 + pools) * nclass, tile), F32),
             sem((10,)),
-            sem((4,)),
-            sem((n_s,)),
-            sem((n_s,)),
-            sem((n_s,)),
-            sem((n_s,)),
-            sem((n_m, 2)),
-            sem((n_m, 2)),
+            sem((n_s,)),
+            sem((n_s,)),
+            sem((n_s,)),
+            sem((n_s,)),
             sem((n_m,)),
             sem((n_m,)),
-            sem((n_s,)),
-            sem((n_s,)),
             sem((n_m,)),
             sem((n_m,)),
+            sem((n_s,)),
+            sem((n_s,)),
+            sem((stage, n_m)),
+            sem((stage, n_m)),
         ],
-        compiler_params=pltpu.CompilerParams(collective_id=0, has_side_effects=True),
+        compiler_params=pltpu.CompilerParams(
+            collective_id=0, has_side_effects=True, vmem_limit_bytes=24 * 1024 * 1024
+        ),
         cost_estimate=pl.CostEstimate(
             flops=2 * blocks * tile * (allrows + nreq), bytes_accessed=2 * blocks * tile, transcendentals=4 * nreq * tile
         ),
         name="inversion",
     )(
-        sensitivity_blocks.reshape(blocks, tile),
-        block_placement_table,
-        needed_tile_lists.T,
-        location_category.reshape(tiles, tile),
-        ground_warmth_celsius,
-        wetness_factor,
-        carbon_reservoirs,
+        pinned(sensitivity_blocks.reshape(blocks, tile)),
+        pinned(block_placement_table),
+        pinned(needed_tile_lists.T),
+        pinned(location_category.reshape(tiles, tile)),
+        pinned(ground_warmth_celsius),
+        pinned(wetness_factor),
+        pinned(carbon_reservoirs),
         category_sensitivity_effect,
         reservoir_decay_effect,
-        category_sensitivity_effect.reshape(1, nclass),
-        reservoir_decay_effect,
-        measured_anomaly,
-        retrieval_precision,
+        pinned(category_sensitivity_effect.reshape(1, nclass)),
+        pinned(reservoir_decay_effect),
+        pinned(measured_anomaly),
+        pinned(retrieval_precision),
     )
     model, grad, classes, cost = pl.pallas_call(
         hand_over,
         out_shape=results,
-        in_specs=[hbm] * 4,
+        in_specs=[vmem] * 4,
         out_specs=(hbm,) * 4,
-        scratch_shapes=[pltpu.VMEM(r.shape, F32) for r in results] + [sem((4,)), sem((4,))],
+        scratch_shapes=[sem((4,))],
         name="results",
     )(*outs)
     return model, grad, classes, cost.reshape(())

time: 31.6 us -> 32.8 us (1.038)
  local copies, waits for them, and re-layouts: 0 us -> 1.77 us
  Pallas kernels: 30.7 us -> 30.2 us
    unnamed x0 -> x6, local copies, waits for them, and re-layouts: none -> 1.77 us
    pallas_call x1, Pallas kernels: 28.6 us -> 28 us  [shards(): pl.pallas_call(functools.partial(kernel, n_s, n_m), out_shape=results, in...]
where the time goes in v4:
time: 32.8 us; the launch traced here: 32.6 us
  Pallas kernels  30.2 us (92%)
  local copies, waits for them, and re-layouts  1.77 us (5%)
  between operations  0.65 us (2%)
    pallas_call x1, Pallas kernels, shards(): pl.pallas_call(functools.partial(kernel, n_s, n_m), out_shape=results, in...  28 us
    pallas_call x1, Pallas kernels, shards(): pl.pallas_call(hand_over, out_shape=results, in_specs=[vmem] * 4, out_spe...  2.14 us
    unnamed x6, local copies, waits for them, and re-layouts  1.77 us

profile of v4, /device:TPU:0, one launch (start us, length us, event | category | flops | bytes accessed | tf_op | source)
XLA Modules:
  0.0 32.6 jit_solution(7812737889581452528)
XLA Ops:
  0.6 28.0 %inversion.1 = (f32[16,128]{1,0:T(8,128)S(1)}, f32[2,8192]{1,0:T(2,128)S(1)}, f32[4,16]{1,0:T(4,128)S(1)}, f32[1,1]{1,0:T(1,128)}) custom-call(bf16[16384,128]{1,0:T(8,128)(2,1)} %bitcast.5, s32[3,128]{1,0:T(4,128)} %table_hbm.1, s32[4,8]{1,0:T(4,128)} %bitcast.7, s32[64,128]{1,0:T(8,128)} %bitcast.6, f32[2,8192]{1,0:T(2,128)} %warm_hbm.1, ...), custom_call_target="tpu_custom_call" | custom-call | flops 402653184 | bytes 4194304 | tf_op jit(solution)/shard_map/inversion/pallas_call | solution.py:365
  28.7 0.0 copy-start
  28.7 0.6 %copy-done = f32[2,8192]{1,0:T(2,128)} copy-done((f32[2,8192]{1,0:T(2,128)}, f32[2,8192]{1,0:T(2,128)S(1)}, u32[]{:S(2)}) %copy-start) | copy-done | bytes 65560
  29.3 0.0 copy-start.1
  29.3 0.6 %copy-done.1 = f32[16,128]{1,0:T(8,128)} copy-done((f32[16,128]{1,0:T(8,128)}, f32[16,128]{1,0:T(8,128)S(1)}, u32[]{:S(2)}) %copy-start.1) | copy-done | bytes 8216
  29.9 0.0 copy-start.2
  29.9 0.6 %copy-done.2 = f32[4,16]{1,0:T(4,128)} copy-done((f32[4,16]{1,0:T(4,128)}, f32[4,16]{1,0:T(4,128)S(1)}, u32[]{:S(2)}) %copy-start.2) | copy-done | bytes 280
  30.4 2.1 %results.1 = (f32[16,128]{1,0:T(8,128)}, f32[2,8192]{1,0:T(2,128)}, f32[4,16]{1,0:T(4,128)}, f32[1,1]{1,0:T(1,128)}) custom-call(f32[16,128]{1,0:T(8,128)} %copy-done.1, f32[2,8192]{1,0:T(2,128)} %copy-done, f32[4,16]{1,0:T(4,128)} %copy-done.2, f32[1,1]{1,0:T(1,128)} %get-tuple-element.15.refs_3_), custom_call_target="tpu_custom_call" | custom-call | tf_op jit(solution)/shard_map/results/pallas_call | solution.py:436
Async XLA Ops:
  28.7 0.6 %copy-start = (f32[2,8192]{1,0:T(2,128)}, f32[2,8192]{1,0:T(2,128)S(1)}, u32[]{:S(2)}) copy-start(f32[2,8192]{1,0:T(2,128)S(1)} %get-tuple-element.13.refs_1_) | copy-start | bytes 196612
  29.3 0.6 %copy-start.1 = (f32[16,128]{1,0:T(8,128)}, f32[16,128]{1,0:T(8,128)S(1)}, u32[]{:S(2)}) copy-start(f32[16,128]{1,0:T(8,128)S(1)} %get-tuple-element.12.refs_0_) | copy-start | bytes 24580
  29.9 0.6 %copy-start.2 = (f32[4,16]{1,0:T(4,128)}, f32[4,16]{1,0:T(4,128)S(1)}, u32[]{:S(2)}) copy-start(f32[4,16]{1,0:T(4,128)S(1)} %get-tuple-element.14.refs_2_) | copy-start | bytes 772

commit v5 on v4

--- a/solution.py
+++ b/solution.py
@@ -439,6 +439,7 @@
         in_specs=[vmem] * 4,
         out_specs=(hbm,) * 4,
         scratch_shapes=[sem((4,))],
+        compiler_params=pltpu.CompilerParams(vmem_limit_bytes=2 * 1024 * 1024),
         name="results",
     )(*outs)
     return model, grad, classes, cost.reshape(())

time: 32.8 us -> 30.2 us (0.921)
  local copies, waits for them, and re-layouts: 1.77 us -> 0 us
  Pallas kernels: 30.2 us -> 29.3 us
    unnamed x6 -> x0, local copies, waits for them, and re-layouts: 1.77 us -> none
    pallas_call x1, Pallas kernels: 2.14 us -> 1.3 us  [shards(): pl.pallas_call(hand_over, out_shape=results, in_specs=[vmem] * 4, out_spe...]
where the time goes in v5:
time: 30.2 us; the launch traced here: 30 us
  Pallas kernels  29.3 us (97%)
  between operations  0.64 us (2%)
    pallas_call x1, Pallas kernels, shards(): pl.pallas_call(functools.partial(kernel, n_s, n_m), out_shape=results, in...  28 us
    pallas_call x1, Pallas kernels, shards(): pl.pallas_call(hand_over, out_shape=results, in_specs=[vmem] * 4, out_spe...  1.3 us

profile of v5, /device:TPU:0, one launch (start us, length us, event | category | flops | bytes accessed | tf_op | source)
XLA Modules:
  0.0 30.0 jit_solution(1403907627295957427)
XLA Ops:
  0.6 28.0 %inversion.1 = (f32[16,128]{1,0:T(8,128)S(1)}, f32[2,8192]{1,0:T(2,128)S(1)}, f32[4,16]{1,0:T(4,128)S(1)}, f32[1,1]{1,0:T(1,128)}) custom-call(bf16[16384,128]{1,0:T(8,128)(2,1)} %bitcast.5, s32[3,128]{1,0:T(4,128)} %table_hbm.1, s32[4,8]{1,0:T(4,128)} %bitcast.7, s32[64,128]{1,0:T(8,128)} %bitcast.6, f32[2,8192]{1,0:T(2,128)} %warm_hbm.1, ...), custom_call_target="tpu_custom_call" | custom-call | flops 402653184 | bytes 4194304 | tf_op jit(solution)/shard_map/inversion/pallas_call | solution.py:365
  28.7 1.3 %results.1 = (f32[16,128]{1,0:T(8,128)}, f32[2,8192]{1,0:T(2,128)}, f32[4,16]{1,0:T(4,128)}, f32[1,1]{1,0:T(1,128)}) custom-call(f32[16,128]{1,0:T(8,128)S(1)} %get-tuple-element.12.refs_0_, f32[2,8192]{1,0:T(2,128)S(1)} %get-tuple-element.13.refs_1_, f32[4,16]{1,0:T(4,128)S(1)} %get-tuple-element.14.refs_2_, f32[1,1]{1,0:T(1,128)} %get-tuple-element.15.refs_3_), custom_call_target="tpu_custom_call" | custom-call | tf_op jit(solution)/shard_map/results/pallas_call | solution.py:436

commit v6 on v5

--- a/solution.py
+++ b/solution.py
@@ -203,14 +203,14 @@
     vb[...] = vecs_b
     loads[9].wait()
 
-    partial = jnp.zeros((allrows, tile), F32)
+    partial = jnp.zeros((tile, allrows), F32)
     for at in range(0, nb, CHUNK):
         left = [
             jnp.where(model_at == rcol[b : b + 1, :], vb[b : b + 1, :], 0.0).astype(BF16) for b in range(at, at + CHUNK)
         ]
         right = [sens[b * tile : (b + 1) * tile, :] for b in range(at, at + CHUNK)]
-        partial += dot(jnp.concatenate(left, axis=1), jnp.concatenate(right, axis=1), ((1,), (1,)))
-    part[0] = partial
+        partial += dot(jnp.concatenate(right, axis=1), jnp.concatenate(left, axis=1), ((1,), (1,)))
+    part[0] = partial.T
 
     swap = [remote(part.at[0], part.at[f], s_p.at[f], r_p.at[f], map_dev(f)) for f in range(1, n_m)]
     for c in swap:

time: 30.2 us -> 30.1 us (level)
  no operation moved by 1% of the time
where the time goes in v6:
time: 30.1 us; the launch traced here: 29.9 us
  Pallas kernels  29.3 us (97%)
  between operations  0.64 us (2%)
    pallas_call x1, Pallas kernels, shards(): pl.pallas_call(functools.partial(kernel, n_s, n_m), out_shape=results, in...  28 us
    pallas_call x1, Pallas kernels, shards(): pl.pallas_call(hand_over, out_shape=results, in_specs=[vmem] * 4, out_spe...  1.3 us

profile of v6, /device:TPU:0, one launch (start us, length us, event | category | flops | bytes accessed | tf_op | source)
XLA Modules:
  0.0 29.9 jit_solution(645287808211739231)
XLA Ops:
  0.6 28.0 %inversion.1 = (f32[16,128]{1,0:T(8,128)S(1)}, f32[2,8192]{1,0:T(2,128)S(1)}, f32[4,16]{1,0:T(4,128)S(1)}, f32[1,1]{1,0:T(1,128)}) custom-call(bf16[16384,128]{1,0:T(8,128)(2,1)} %bitcast.5, s32[3,128]{1,0:T(4,128)} %table_hbm.1, s32[4,8]{1,0:T(4,128)} %bitcast.7, s32[64,128]{1,0:T(8,128)} %bitcast.6, f32[2,8192]{1,0:T(2,128)} %warm_hbm.1, ...), custom_call_target="tpu_custom_call" | custom-call | flops 402653184 | bytes 4194304 | tf_op jit(solution)/shard_map/inversion/pallas_call | solution.py:365
  28.6 1.3 %results.1 = (f32[16,128]{1,0:T(8,128)}, f32[2,8192]{1,0:T(2,128)}, f32[4,16]{1,0:T(4,128)}, f32[1,1]{1,0:T(1,128)}) custom-call(f32[16,128]{1,0:T(8,128)S(1)} %get-tuple-element.12.refs_0_, f32[2,8192]{1,0:T(2,128)S(1)} %get-tuple-element.13.refs_1_, f32[4,16]{1,0:T(4,128)S(1)} %get-tuple-element.14.refs_2_, f32[1,1]{1,0:T(1,128)} %get-tuple-element.15.refs_3_), custom_call_target="tpu_custom_call" | custom-call | tf_op jit(solution)/shard_map/results/pallas_call | solution.py:436
